TPU v7x, 256 devices: a whole 4x4x8 slice. The times are simulated.
256 devices in a mesh: grp: 8 (over x, core), row: 32 (over y, z).
Axes of the slice: x: 4, y: 4, z: 8, core: 2. Of those that a mesh axis runs over, the one named last changes fastest.
Arguments:
- features: bfloat16 [8192, 8192], P('row', 'grp'), may hold values from -0.0625 to 0.0625
- residual: float32 [8192, 576], P('row'), may hold values from -6 to 6
- precond: float32 [8192, 1024], P('grp'), as said below
Outputs:
- coefs: float32 [8192, 576], P('grp')
- section_resid: float32 [8, 8192, 576], P('grp', 'row')
Inputs may be any that keep to these rules, and one draw needn't show every extreme that they name: Each 1024 x 1024 block of precond is symmetric and positive definite.
All inputs are finite; a program needn't handle non-finite values.
Results may differ from a plain program's by a relative error of at most 0.009.
Values may be sent and summed in bfloat16 or wider, within the bound.
A program may use at most 64 MiB of HBM per device.

v0:
```python
import jax
import jax.numpy as jnp
from jax import lax
from jax.sharding import PartitionSpec as P


def from_behind(block, axis, distance):
    devices = range(lax.axis_size(axis))
    route = [(i - distance, i) for i in devices if i - distance in devices]
    return lax.ppermute(block, axis, route)


def chain_sweep(features, residual, precond):
    section_index = lax.axis_index("grp")
    section_count = lax.axis_size("grp")
    row_count, target_width = residual.shape
    block_width = features.shape[1]
    panel_count = 3
    panel_width = target_width // panel_count
    step_count = section_count + panel_count - 1

    def correlate(rounded):
        correlation = lax.dot_general(
            features, rounded, (((0,), (0,)), ((), ())), preferred_element_type=jnp.float32
        )
        correlation = lax.psum(correlation, "row")
        share = block_width // lax.axis_size("row")
        first = lax.axis_index("row") * share
        own_map = lax.dynamic_slice_in_dim(precond, first, share, 0)
        own_rows = jnp.dot(own_map, correlation, precision=lax.Precision.HIGHEST)
        return lax.all_gather(own_rows, "row", axis=0, tiled=True)

    def turn(turn_index, loop_state):
        current, coef_table, resid_table = loop_state
        position = turn_index - section_index
        inside = jnp.logical_and(position >= 0, position < panel_count)
        panel_slot = jnp.clip(position, 0, panel_count - 1) * panel_width
        fresh_panel = lax.dynamic_slice_in_dim(residual, panel_slot, panel_width, 1)
        current = jnp.where(section_index == 0, fresh_panel, current)
        rounded = current.astype(jnp.bfloat16)
        coefficient = correlate(rounded)
        updated = current - jnp.dot(
            features, coefficient.astype(jnp.bfloat16), preferred_element_type=jnp.float32
        )
        old_coef = lax.dynamic_slice_in_dim(coef_table, panel_slot, panel_width, 1)
        coef_table = lax.dynamic_update_slice_in_dim(
            coef_table, jnp.where(inside, coefficient, old_coef), panel_slot, 1
        )
        old_resid = lax.dynamic_slice_in_dim(resid_table, panel_slot, panel_width, 2)
        resid_table = lax.dynamic_update_slice_in_dim(
            resid_table, jnp.where(inside, updated[None], old_resid), panel_slot, 2
        )
        passed = from_behind(updated, "grp", 1)
        return (passed, coef_table, resid_table)

    start_state = (
        jnp.zeros((row_count, panel_width), jnp.float32),
        jnp.zeros((block_width, target_width), jnp.float32),
        jnp.zeros((1, row_count, target_width), jnp.float32),
    )
    final_state = lax.fori_loop(0, step_count, turn, start_state)
    return (final_state[1], final_state[2])


def local(features, residual, precond):
    return chain_sweep(features, residual, precond)


def solution(mesh):
    placed = (P("row", "grp"), P("row", None), P("grp", None))
    return jax.shard_map(
        local,
        mesh=mesh,
        in_specs=placed,
        out_specs=(P("grp", None), P("grp", "row", None)),
        check_vma=False,
    )
```

profile of v0, /device:TPU:1, one launch (start us, length us, event | category | flops | bytes accessed | tf_op | source)
XLA Modules:
  0.0 2120.8 jit_solution(15154932183782905294)
XLA Ops:
  9.8 2104.2 %while.18 = (s32[]{:T(128)}, f32[256,192]{0,1:T(8,128)S(1)}, f32[1024,576]{0,1:T(8,128)}, f32[1,256,576]{1,2,0:T(8,128)}, pred[]{:T(512)}, /*index=5*/s32[]{:T(1...) while((s32[]{:T(128)}, f32[256,192]{0,1:T(8,128)S(1)}, ...), condition=%wide.region_2.3_spmd, body=%wide.region_0.2_spmd.sunk | while | flops 277610496 | bytes 19809716 | solution.py:61
  9.8 2.1 convolution_bitcast_fusion.3
  13.4 148.3 %all-reduce.2.cloned.1.call-done = f32[1024,192]{0,1:T(8,128)} async-done(((f32[1024,192]{0,1:T(8,128)}), f32[1024,192]{0,1:T(8,128)}) %all-reduce.2.cloned.1.call-update) | async-done | bytes 786448 | tf_op jit(solution)/shard_map/while/body/eval_jaxpr/psum | solution.py:26
  163.7 36.9 %all_gather.9 = f32[1024,192]{1,0:T(8,128)S(1)} all-gather(f32[32,192]{1,0:T(8,128)S(1)} %fusion.23), channel_id=1, replica_groups=mesh['grp'=8,'row'=32] {'row'}, dimensions={0}, use_global_device_ids=true | all-gather | bytes 811008 | tf_op jit(solution)/shard_map/while/body/eval_jaxpr/all_gather | solution.py:31
  200.6 2.0 fusion.24
  202.7 20.0 collective-permute-start
  225.3 2.1 convolution_bitcast_fusion.3
  228.9 142.8 %all-reduce.2.cloned.1.call-done = f32[1024,192]{0,1:T(8,128)} async-done(((f32[1024,192]{0,1:T(8,128)}), f32[1024,192]{0,1:T(8,128)}) %all-reduce.2.cloned.1.call-update) | async-done | bytes 786448 | tf_op jit(solution)/shard_map/while/body/eval_jaxpr/psum | solution.py:26
  373.7 36.9 %all_gather.9 = f32[1024,192]{1,0:T(8,128)S(1)} all-gather(f32[32,192]{1,0:T(8,128)S(1)} %fusion.23), channel_id=1, replica_groups=mesh['grp'=8,'row'=32] {'row'}, dimensions={0}, use_global_device_ids=true | all-gather | bytes 811008 | tf_op jit(solution)/shard_map/while/body/eval_jaxpr/all_gather | solution.py:31
  410.6 2.0 fusion.24
  412.7 20.0 collective-permute-start
  435.3 2.1 convolution_bitcast_fusion.3
  438.9 142.8 %all-reduce.2.cloned.1.call-done = f32[1024,192]{0,1:T(8,128)} async-done(((f32[1024,192]{0,1:T(8,128)}), f32[1024,192]{0,1:T(8,128)}) %all-reduce.2.cloned.1.call-update) | async-done | bytes 786448 | tf_op jit(solution)/shard_map/while/body/eval_jaxpr/psum | solution.py:26
  583.7 36.9 %all_gather.9 = f32[1024,192]{1,0:T(8,128)S(1)} all-gather(f32[32,192]{1,0:T(8,128)S(1)} %fusion.23), channel_id=1, replica_groups=mesh['grp'=8,'row'=32] {'row'}, dimensions={0}, use_global_device_ids=true | all-gather | bytes 811008 | tf_op jit(solution)/shard_map/while/body/eval_jaxpr/all_gather | solution.py:31
  620.6 2.0 fusion.24
  622.7 20.0 collective-permute-start
  645.3 2.1 convolution_bitcast_fusion.3
  648.9 142.4 %all-reduce.2.cloned.1.call-done = f32[1024,192]{0,1:T(8,128)} async-done(((f32[1024,192]{0,1:T(8,128)}), f32[1024,192]{0,1:T(8,128)}) %all-reduce.2.cloned.1.call-update) | async-done | bytes 786448 | tf_op jit(solution)/shard_map/while/body/eval_jaxpr/psum | solution.py:26
  793.4 36.9 %all_gather.9 = f32[1024,192]{1,0:T(8,128)S(1)} all-gather(f32[32,192]{1,0:T(8,128)S(1)} %fusion.23), channel_id=1, replica_groups=mesh['grp'=8,'row'=32] {'row'}, dimensions={0}, use_global_device_ids=true | all-gather | bytes 811008 | tf_op jit(solution)/shard_map/while/body/eval_jaxpr/all_gather | solution.py:31
  830.3 2.0 fusion.24
  832.4 20.0 collective-permute-start
  855.0 2.1 convolution_bitcast_fusion.3
  858.6 142.4 %all-reduce.2.cloned.1.call-done = f32[1024,192]{0,1:T(8,128)} async-done(((f32[1024,192]{0,1:T(8,128)}), f32[1024,192]{0,1:T(8,128)}) %all-reduce.2.cloned.1.call-update) | async-done | bytes 786448 | tf_op jit(solution)/shard_map/while/body/eval_jaxpr/psum | solution.py:26
  1003.1 36.9 %all_gather.9 = f32[1024,192]{1,0:T(8,128)S(1)} all-gather(f32[32,192]{1,0:T(8,128)S(1)} %fusion.23), channel_id=1, replica_groups=mesh['grp'=8,'row'=32] {'row'}, dimensions={0}, use_global_device_ids=true | all-gather | bytes 811008 | tf_op jit(solution)/shard_map/while/body/eval_jaxpr/all_gather | solution.py:31
  1040.0 2.0 fusion.24
  1042.1 20.0 collective-permute-start
  1064.7 2.1 convolution_bitcast_fusion.3
  1068.3 142.5 %all-reduce.2.cloned.1.call-done = f32[1024,192]{0,1:T(8,128)} async-done(((f32[1024,192]{0,1:T(8,128)}), f32[1024,192]{0,1:T(8,128)}) %all-reduce.2.cloned.1.call-update) | async-done | bytes 786448 | tf_op jit(solution)/shard_map/while/body/eval_jaxpr/psum | solution.py:26
  1212.8 36.9 %all_gather.9 = f32[1024,192]{1,0:T(8,128)S(1)} all-gather(f32[32,192]{1,0:T(8,128)S(1)} %fusion.23), channel_id=1, replica_groups=mesh['grp'=8,'row'=32] {'row'}, dimensions={0}, use_global_device_ids=true | all-gather | bytes 811008 | tf_op jit(solution)/shard_map/while/body/eval_jaxpr/all_gather | solution.py:31
  1249.7 2.0 fusion.24
  1251.8 20.0 collective-permute-start
  1274.4 2.1 convolution_bitcast_fusion.3
  1278.0 142.8 %all-reduce.2.cloned.1.call-done = f32[1024,192]{0,1:T(8,128)} async-done(((f32[1024,192]{0,1:T(8,128)}), f32[1024,192]{0,1:T(8,128)}) %all-reduce.2.cloned.1.call-update) | async-done | bytes 786448 | tf_op jit(solution)/shard_map/while/body/eval_jaxpr/psum | solution.py:26
  1422.8 36.9 %all_gather.9 = f32[1024,192]{1,0:T(8,128)S(1)} all-gather(f32[32,192]{1,0:T(8,128)S(1)} %fusion.23), channel_id=1, replica_groups=mesh['grp'=8,'row'=32] {'row'}, dimensions={0}, use_global_device_ids=true | all-gather | bytes 811008 | tf_op jit(solution)/shard_map/while/body/eval_jaxpr/all_gather | solution.py:31
  1461.8 20.0 collective-permute-start
  1484.4 2.1 convolution_bitcast_fusion.3
  1488.0 142.7 %all-reduce.2.cloned.1.call-done = f32[1024,192]{0,1:T(8,128)} async-done(((f32[1024,192]{0,1:T(8,128)}), f32[1024,192]{0,1:T(8,128)}) %all-reduce.2.cloned.1.call-update) | async-done | bytes 786448 | tf_op jit(solution)/shard_map/while/body/eval_jaxpr/psum | solution.py:26
  1632.8 36.9 %all_gather.9 = f32[1024,192]{1,0:T(8,128)S(1)} all-gather(f32[32,192]{1,0:T(8,128)S(1)} %fusion.23), channel_id=1, replica_groups=mesh['grp'=8,'row'=32] {'row'}, dimensions={0}, use_global_device_ids=true | all-gather | bytes 811008 | tf_op jit(solution)/shard_map/while/body/eval_jaxpr/all_gather | solution.py:31
  1671.7 20.0 collective-permute-start
  1694.3 2.1 convolution_bitcast_fusion.3
  1698.0 142.8 %all-reduce.2.cloned.1.call-done = f32[1024,192]{0,1:T(8,128)} async-done(((f32[1024,192]{0,1:T(8,128)}), f32[1024,192]{0,1:T(8,128)}) %all-reduce.2.cloned.1.call-update) | async-done | bytes 786448 | tf_op jit(solution)/shard_map/while/body/eval_jaxpr/psum | solution.py:26
  1842.8 36.9 %all_gather.9 = f32[1024,192]{1,0:T(8,128)S(1)} all-gather(f32[32,192]{1,0:T(8,128)S(1)} %fusion.23), channel_id=1, replica_groups=mesh['grp'=8,'row'=32] {'row'}, dimensions={0}, use_global_device_ids=true | all-gather | bytes 811008 | tf_op jit(solution)/shard_map/while/body/eval_jaxpr/all_gather | solution.py:31
  1881.8 20.0 collective-permute-start
  1904.3 2.1 convolution_bitcast_fusion.3
  1908.0 142.4 %all-reduce.2.cloned.1.call-done = f32[1024,192]{0,1:T(8,128)} async-done(((f32[1024,192]{0,1:T(8,128)}), f32[1024,192]{0,1:T(8,128)}) %all-reduce.2.cloned.1.call-update) | async-done | bytes 786448 | tf_op jit(solution)/shard_map/while/body/eval_jaxpr/psum | solution.py:26
  2052.5 36.9 %all_gather.9 = f32[1024,192]{1,0:T(8,128)S(1)} all-gather(f32[32,192]{1,0:T(8,128)S(1)} %fusion.23), channel_id=1, replica_groups=mesh['grp'=8,'row'=32] {'row'}, dimensions={0}, use_global_device_ids=true | all-gather | bytes 811008 | tf_op jit(solution)/shard_map/while/body/eval_jaxpr/all_gather | solution.py:31
  2089.4 2.0 fusion.24
  2091.4 20.0 collective-permute-start
  (98 shorter events, 70.2 us)
Async XLA Ops:
  7.2 2.6 copy-start
  9.8 151.9 %all-reduce.2.cloned.1.call-start = ((), (), s32[]{:S(2)}) async-start(), calls=%async_computation | async-start | bytes 1572864 | tf_op jit(solution)/shard_map/while/body/eval_jaxpr/psum | solution.py:26
  202.7 22.6 %collective-permute-start = (f32[256,192]{0,1:T(8,128)S(1)}, f32[256,192]{0,1:T(8,128)S(1)}, u32[]{:S(2)}, u32[]{:S(2)}) collective-permute-start(f32[256,192]{0,1:T(8,128)S(1)} %get-tuple-element.260), channel_id=1, source_target_pairs={{0,32},{32,64},{64,96},{96,128},{128,160},{160,192},{192,224},{1,3... | collective-permute-start | bytes 589832 | tf_op jit(solution)/shard_map/while/body/eval_jaxpr/ppermute | solution.py:10
  225.3 146.4 %all-reduce.2.cloned.1.call-start = ((), (), s32[]{:S(2)}) async-start(), calls=%async_computation | async-start | bytes 1572864 | tf_op jit(solution)/shard_map/while/body/eval_jaxpr/psum | solution.py:26
  412.7 22.6 %collective-permute-start = (f32[256,192]{0,1:T(8,128)S(1)}, f32[256,192]{0,1:T(8,128)S(1)}, u32[]{:S(2)}, u32[]{:S(2)}) collective-permute-start(f32[256,192]{0,1:T(8,128)S(1)} %get-tuple-element.260), channel_id=1, source_target_pairs={{0,32},{32,64},{64,96},{96,128},{128,160},{160,192},{192,224},{1,3... | collective-permute-start | bytes 589832 | tf_op jit(solution)/shard_map/while/body/eval_jaxpr/ppermute | solution.py:10
  435.3 146.4 %all-reduce.2.cloned.1.call-start = ((), (), s32[]{:S(2)}) async-start(), calls=%async_computation | async-start | bytes 1572864 | tf_op jit(solution)/shard_map/while/body/eval_jaxpr/psum | solution.py:26
  622.7 22.6 %collective-permute-start = (f32[256,192]{0,1:T(8,128)S(1)}, f32[256,192]{0,1:T(8,128)S(1)}, u32[]{:S(2)}, u32[]{:S(2)}) collective-permute-start(f32[256,192]{0,1:T(8,128)S(1)} %get-tuple-element.260), channel_id=1, source_target_pairs={{0,32},{32,64},{64,96},{96,128},{128,160},{160,192},{192,224},{1,3... | collective-permute-start | bytes 589832 | tf_op jit(solution)/shard_map/while/body/eval_jaxpr/ppermute | solution.py:10
  645.3 146.1 %all-reduce.2.cloned.1.call-start = ((), (), s32[]{:S(2)}) async-start(), calls=%async_computation | async-start | bytes 1572864 | tf_op jit(solution)/shard_map/while/body/eval_jaxpr/psum | solution.py:26
  832.4 22.6 %collective-permute-start = (f32[256,192]{0,1:T(8,128)S(1)}, f32[256,192]{0,1:T(8,128)S(1)}, u32[]{:S(2)}, u32[]{:S(2)}) collective-permute-start(f32[256,192]{0,1:T(8,128)S(1)} %get-tuple-element.260), channel_id=1, source_target_pairs={{0,32},{32,64},{64,96},{96,128},{128,160},{160,192},{192,224},{1,3... | collective-permute-start | bytes 589832 | tf_op jit(solution)/shard_map/while/body/eval_jaxpr/ppermute | solution.py:10
  855.0 146.1 %all-reduce.2.cloned.1.call-start = ((), (), s32[]{:S(2)}) async-start(), calls=%async_computation | async-start | bytes 1572864 | tf_op jit(solution)/shard_map/while/body/eval_jaxpr/psum | solution.py:26
  1042.1 22.6 %collective-permute-start = (f32[256,192]{0,1:T(8,128)S(1)}, f32[256,192]{0,1:T(8,128)S(1)}, u32[]{:S(2)}, u32[]{:S(2)}) collective-permute-start(f32[256,192]{0,1:T(8,128)S(1)} %get-tuple-element.260), channel_id=1, source_target_pairs={{0,32},{32,64},{64,96},{96,128},{128,160},{160,192},{192,224},{1,3... | collective-permute-start | bytes 589832 | tf_op jit(solution)/shard_map/while/body/eval_jaxpr/ppermute | solution.py:10
  1064.7 146.1 %all-reduce.2.cloned.1.call-start = ((), (), s32[]{:S(2)}) async-start(), calls=%async_computation | async-start | bytes 1572864 | tf_op jit(solution)/shard_map/while/body/eval_jaxpr/psum | solution.py:26
  1251.8 22.6 %collective-permute-start = (f32[256,192]{0,1:T(8,128)S(1)}, f32[256,192]{0,1:T(8,128)S(1)}, u32[]{:S(2)}, u32[]{:S(2)}) collective-permute-start(f32[256,192]{0,1:T(8,128)S(1)} %get-tuple-element.260), channel_id=1, source_target_pairs={{0,32},{32,64},{64,96},{96,128},{128,160},{160,192},{192,224},{1,3... | collective-permute-start | bytes 589832 | tf_op jit(solution)/shard_map/while/body/eval_jaxpr/ppermute | solution.py:10
  1274.4 146.4 %all-reduce.2.cloned.1.call-start = ((), (), s32[]{:S(2)}) async-start(), calls=%async_computation | async-start | bytes 1572864 | tf_op jit(solution)/shard_map/while/body/eval_jaxpr/psum | solution.py:26
  1461.8 22.6 %collective-permute-start = (f32[256,192]{0,1:T(8,128)S(1)}, f32[256,192]{0,1:T(8,128)S(1)}, u32[]{:S(2)}, u32[]{:S(2)}) collective-permute-start(f32[256,192]{0,1:T(8,128)S(1)} %get-tuple-element.260), channel_id=1, source_target_pairs={{0,32},{32,64},{64,96},{96,128},{128,160},{160,192},{192,224},{1,3... | collective-permute-start | bytes 589832 | tf_op jit(solution)/shard_map/while/body/eval_jaxpr/ppermute | solution.py:10
  1484.4 146.4 %all-reduce.2.cloned.1.call-start = ((), (), s32[]{:S(2)}) async-start(), calls=%async_computation | async-start | bytes 1572864 | tf_op jit(solution)/shard_map/while/body/eval_jaxpr/psum | solution.py:26
  1671.7 22.6 %collective-permute-start = (f32[256,192]{0,1:T(8,128)S(1)}, f32[256,192]{0,1:T(8,128)S(1)}, u32[]{:S(2)}, u32[]{:S(2)}) collective-permute-start(f32[256,192]{0,1:T(8,128)S(1)} %get-tuple-element.260), channel_id=1, source_target_pairs={{0,32},{32,64},{64,96},{96,128},{128,160},{160,192},{192,224},{1,3... | collective-permute-start | bytes 589832 | tf_op jit(solution)/shard_map/while/body/eval_jaxpr/ppermute | solution.py:10
  1694.3 146.4 %all-reduce.2.cloned.1.call-start = ((), (), s32[]{:S(2)}) async-start(), calls=%async_computation | async-start | bytes 1572864 | tf_op jit(solution)/shard_map/while/body/eval_jaxpr/psum | solution.py:26
  1881.8 22.6 %collective-permute-start = (f32[256,192]{0,1:T(8,128)S(1)}, f32[256,192]{0,1:T(8,128)S(1)}, u32[]{:S(2)}, u32[]{:S(2)}) collective-permute-start(f32[256,192]{0,1:T(8,128)S(1)} %get-tuple-element.260), channel_id=1, source_target_pairs={{0,32},{32,64},{64,96},{96,128},{128,160},{160,192},{192,224},{1,3... | collective-permute-start | bytes 589832 | tf_op jit(solution)/shard_map/while/body/eval_jaxpr/ppermute | solution.py:10
  1904.3 146.1 %all-reduce.2.cloned.1.call-start = ((), (), s32[]{:S(2)}) async-start(), calls=%async_computation | async-start | bytes 1572864 | tf_op jit(solution)/shard_map/while/body/eval_jaxpr/psum | solution.py:26
  2091.4 22.6 %collective-permute-start = (f32[256,192]{0,1:T(8,128)S(1)}, f32[256,192]{0,1:T(8,128)S(1)}, u32[]{:S(2)}, u32[]{:S(2)}) collective-permute-start(f32[256,192]{0,1:T(8,128)S(1)} %get-tuple-element.260), channel_id=1, source_target_pairs={{0,32},{32,64},{64,96},{96,128},{128,160},{160,192},{192,224},{1,3... | collective-permute-start | bytes 589832 | tf_op jit(solution)/shard_map/while/body/eval_jaxpr/ppermute | solution.py:10
Sparse Core Ops, SparseCore 0:
  13.9 147.6 all-reduce.1
  229.4 142.1 all-reduce.1
  439.4 142.2 all-reduce.1
  649.1 142.1 all-reduce.1
  858.8 142.1 all-reduce.1
  1068.5 142.2 all-reduce.1
  1278.5 142.1 all-reduce.1
  1488.5 142.1 all-reduce.1
  1698.5 142.2 all-reduce.1
  1908.2 142.1 all-reduce.1
where the time goes:
time: 2120 us
  waiting for transfers between devices  1440 us (68%)
  blocking collectives  369 us (17%)
  starting transfers between devices  200 us (9%)
  matrix products  61.7 us (3%)
  local copies, waits for them, and re-layouts  30.3 us (1%)
    psum x10, waiting for transfers between devices, correlate(): correlation = lax.psum(correlation, 'row')  1430 us
    all_gather x10, blocking collectives, correlate(): return lax.all_gather(own_rows, 'row', axis=0, tiled=True)  369 us
    ppermute x10, starting transfers between devices, from_behind(): return lax.ppermute(block, axis, route)  200 us
  transfers between devices with their start and end apart: 20, of which 20 were waited for; matrix products, arithmetic and copies ran while one was open for 1% of the time, Pallas kernels for 0%

commit v1 on v0

--- a/solution.py
+++ b/solution.py
@@ -28,7 +28,9 @@
         first = lax.axis_index("row") * share
         own_map = lax.dynamic_slice_in_dim(precond, first, share, 0)
         own_rows = jnp.dot(own_map, correlation, precision=lax.Precision.HIGHEST)
-        return lax.all_gather(own_rows, "row", axis=0, tiled=True)
+        return jnp.concatenate(
+            lax.all_to_all(jnp.stack([own_rows] * lax.axis_size("row")), "row", 0, 0), axis=0
+        )
 
     def turn(turn_index, loop_state):
         current, coef_table, resid_table = loop_state

time: 2120 us -> 1940 us (0.915)
  blocking collectives: 369 us -> 0 us
  waiting for transfers between devices: 1440 us -> 1630 us
    all_gather x10 -> x0, blocking collectives: 369 us -> none  [correlate(): return lax.all_gather(own_rows, 'row', axis=0, tiled=True)]
    all_to_all x0 -> x10, waiting for transfers between devices: none -> 180 us  [correlate(): lax.all_to_all(jnp.stack([own_rows] * lax.axis_size('row')), 'row', 0, 0)]
    ppermute x10, starting transfers between devices: 200 us -> 129 us  [from_behind(): return lax.ppermute(block, axis, route)]
    all_to_all x0 -> x10, starting transfers between devices: none -> 57.4 us  [correlate(): lax.all_to_all(jnp.stack([own_rows] * lax.axis_size('row')), 'row', 0, 0)]
  transfers between devices with their start and end apart: 20 -> 30, of which waited for: 20 -> 30; matrix products, arithmetic and copies ran while one was open for 1% -> 2% of each run, Pallas kernels for 0% -> 0%
where the time goes in v1:
time: 1940 us
  waiting for transfers between devices  1630 us (84%)
  starting transfers between devices  186 us (10%)
  matrix products  65.5 us (3%)
  local copies, waits for them, and re-layouts  41.2 us (2%)
    psum x10, waiting for transfers between devices, correlate(): correlation = lax.psum(correlation, 'row')  1440 us
    all_to_all x10, waiting for transfers between devices, correlate(): lax.all_to_all(jnp.stack([own_rows] * lax.axis_size('row')), 'row', 0, 0)  180 us
    ppermute x10, starting transfers between devices, from_behind(): return lax.ppermute(block, axis, route)  129 us
    all_to_all x10, starting transfers between devices, correlate(): lax.all_to_all(jnp.stack([own_rows] * lax.axis_size('row')), 'row', 0, 0)  57.4 us
  transfers between devices with their start and end apart: 30, of which 30 were waited for; matrix products, arithmetic and copies ran while one was open for 2% of the time, Pallas kernels for 0%

profile of v1, /device:TPU:1, one launch (start us, length us, event | category | flops | bytes accessed | tf_op | source)
XLA Modules:
  0.0 1938.1 jit_solution(5775858698260720273)
XLA Ops:
  9.7 1921.5 %while.18 = (s32[]{:T(128)}, f32[256,192]{0,1:T(8,128)S(1)}, f32[1024,576]{0,1:T(8,128)}, f32[1,256,576]{1,2,0:T(8,128)}, pred[]{:T(512)}, /*index=5*/s32[]{:T(1...) while((s32[]{:T(128)}, f32[256,192]{0,1:T(8,128)S(1)}, ...), condition=%wide.region_2.3_spmd, body=%wide.region_0.2_spmd.sunk | while | flops 277610496 | bytes 23479764 | solution.py:63
  12.1 149.6 %all-reduce.2.cloned.1.call-done = f32[1024,192]{0,1:T(8,128)} async-done(((f32[1024,192]{0,1:T(8,128)}), f32[1024,192]{0,1:T(8,128)}) %all-reduce.2.cloned.1.call-update) | async-done | bytes 786448 | tf_op jit(solution)/shard_map/while/body/eval_jaxpr/psum | solution.py:26
  164.8 5.7 all-to-all-start
  172.1 17.9 all-to-all-done
  192.3 12.9 collective-permute-start
  207.8 2.3 convolution_bitcast_fusion.3
  210.1 143.2 %all-reduce.2.cloned.1.call-done = f32[1024,192]{0,1:T(8,128)} async-done(((f32[1024,192]{0,1:T(8,128)}), f32[1024,192]{0,1:T(8,128)}) %all-reduce.2.cloned.1.call-update) | async-done | bytes 786448 | tf_op jit(solution)/shard_map/while/body/eval_jaxpr/psum | solution.py:26
  356.4 5.7 all-to-all-start
  363.7 18.0 all-to-all-done
  384.0 12.9 collective-permute-start
  399.5 2.3 convolution_bitcast_fusion.3
  401.8 143.1 %all-reduce.2.cloned.1.call-done = f32[1024,192]{0,1:T(8,128)} async-done(((f32[1024,192]{0,1:T(8,128)}), f32[1024,192]{0,1:T(8,128)}) %all-reduce.2.cloned.1.call-update) | async-done | bytes 786448 | tf_op jit(solution)/shard_map/while/body/eval_jaxpr/psum | solution.py:26
  548.1 5.7 all-to-all-start
  555.3 18.0 all-to-all-done
  575.6 12.9 collective-permute-start
  591.0 2.3 convolution_bitcast_fusion.3
  593.4 142.8 %all-reduce.2.cloned.1.call-done = f32[1024,192]{0,1:T(8,128)} async-done(((f32[1024,192]{0,1:T(8,128)}), f32[1024,192]{0,1:T(8,128)}) %all-reduce.2.cloned.1.call-update) | async-done | bytes 786448 | tf_op jit(solution)/shard_map/while/body/eval_jaxpr/psum | solution.py:26
  739.3 5.7 all-to-all-start
  746.6 18.0 all-to-all-done
  766.9 12.9 collective-permute-start
  782.3 2.3 convolution_bitcast_fusion.3
  784.7 142.8 %all-reduce.2.cloned.1.call-done = f32[1024,192]{0,1:T(8,128)} async-done(((f32[1024,192]{0,1:T(8,128)}), f32[1024,192]{0,1:T(8,128)}) %all-reduce.2.cloned.1.call-update) | async-done | bytes 786448 | tf_op jit(solution)/shard_map/while/body/eval_jaxpr/psum | solution.py:26
  930.7 5.7 all-to-all-start
  938.0 18.0 all-to-all-done
  958.2 12.9 collective-permute-start
  973.7 2.3 convolution_bitcast_fusion.3
  976.0 142.8 %all-reduce.2.cloned.1.call-done = f32[1024,192]{0,1:T(8,128)} async-done(((f32[1024,192]{0,1:T(8,128)}), f32[1024,192]{0,1:T(8,128)}) %all-reduce.2.cloned.1.call-update) | async-done | bytes 786448 | tf_op jit(solution)/shard_map/while/body/eval_jaxpr/psum | solution.py:26
  1122.0 5.7 all-to-all-start
  1129.3 17.9 all-to-all-done
  1149.5 12.9 collective-permute-start
  1167.3 143.2 %all-reduce.2.cloned.1.call-done = f32[1024,192]{0,1:T(8,128)} async-done(((f32[1024,192]{0,1:T(8,128)}), f32[1024,192]{0,1:T(8,128)}) %all-reduce.2.cloned.1.call-update) | async-done | bytes 786448 | tf_op jit(solution)/shard_map/while/body/eval_jaxpr/psum | solution.py:26
  1313.6 5.7 all-to-all-start
  1320.9 18.0 all-to-all-done
  1341.2 12.9 collective-permute-start
  1356.6 2.3 convolution_bitcast_fusion.3
  1359.0 143.2 %all-reduce.2.cloned.1.call-done = f32[1024,192]{0,1:T(8,128)} async-done(((f32[1024,192]{0,1:T(8,128)}), f32[1024,192]{0,1:T(8,128)}) %all-reduce.2.cloned.1.call-update) | async-done | bytes 786448 | tf_op jit(solution)/shard_map/while/body/eval_jaxpr/psum | solution.py:26
  1505.3 5.7 all-to-all-start
  1512.6 18.0 all-to-all-done
  1532.8 12.9 collective-permute-start
  1550.6 143.2 %all-reduce.2.cloned.1.call-done = f32[1024,192]{0,1:T(8,128)} async-done(((f32[1024,192]{0,1:T(8,128)}), f32[1024,192]{0,1:T(8,128)}) %all-reduce.2.cloned.1.call-update) | async-done | bytes 786448 | tf_op jit(solution)/shard_map/while/body/eval_jaxpr/psum | solution.py:26
  1696.9 5.7 all-to-all-start
  1704.2 18.0 all-to-all-done
  1724.4 12.9 collective-permute-start
  1739.9 2.3 convolution_bitcast_fusion.3
  1742.3 142.8 %all-reduce.2.cloned.1.call-done = f32[1024,192]{0,1:T(8,128)} async-done(((f32[1024,192]{0,1:T(8,128)}), f32[1024,192]{0,1:T(8,128)}) %all-reduce.2.cloned.1.call-update) | async-done | bytes 786448 | tf_op jit(solution)/shard_map/while/body/eval_jaxpr/psum | solution.py:26
  1888.2 5.7 all-to-all-start
  1895.5 18.0 all-to-all-done
  1915.8 12.9 collective-permute-start
  (126 shorter events, 104.5 us)
Async XLA Ops:
  9.7 151.9 %all-reduce.2.cloned.1.call-start = ((), (), s32[]{:S(2)}) async-start(), calls=%async_computation.1 | async-start | bytes 1572864 | tf_op jit(solution)/shard_map/while/body/eval_jaxpr/psum | solution.py:26
  164.8 25.2 %all-to-all-start = ((f32[32,32,192]{2,1,0:T(8,128)}), f32[32,32,192]{2,1,0:T(8,128)S(1)}, u32[]{:S(2)}, u32[]{:S(2)}) async-start(f32[32,32,192]{2,1,0:T(8,128)} %stack.7), calls=%async_computation | async-start | bytes 2097152 | tf_op jit(solution)/shard_map/while/body/eval_jaxpr/all_to_all | solution.py:32
  192.3 15.5 collective-permute-start
  207.8 145.5 %all-reduce.2.cloned.1.call-start = ((), (), s32[]{:S(2)}) async-start(), calls=%async_computation.1 | async-start | bytes 1572864 | tf_op jit(solution)/shard_map/while/body/eval_jaxpr/psum | solution.py:26
  356.4 25.3 %all-to-all-start = ((f32[32,32,192]{2,1,0:T(8,128)}), f32[32,32,192]{2,1,0:T(8,128)S(1)}, u32[]{:S(2)}, u32[]{:S(2)}) async-start(f32[32,32,192]{2,1,0:T(8,128)} %stack.7), calls=%async_computation | async-start | bytes 2097152 | tf_op jit(solution)/shard_map/while/body/eval_jaxpr/all_to_all | solution.py:32
  384.0 15.5 collective-permute-start
  399.4 145.5 %all-reduce.2.cloned.1.call-start = ((), (), s32[]{:S(2)}) async-start(), calls=%async_computation.1 | async-start | bytes 1572864 | tf_op jit(solution)/shard_map/while/body/eval_jaxpr/psum | solution.py:26
  548.1 25.3 %all-to-all-start = ((f32[32,32,192]{2,1,0:T(8,128)}), f32[32,32,192]{2,1,0:T(8,128)S(1)}, u32[]{:S(2)}, u32[]{:S(2)}) async-start(f32[32,32,192]{2,1,0:T(8,128)} %stack.7), calls=%async_computation | async-start | bytes 2097152 | tf_op jit(solution)/shard_map/while/body/eval_jaxpr/all_to_all | solution.py:32
  575.6 15.5 collective-permute-start
  591.0 145.2 %all-reduce.2.cloned.1.call-start = ((), (), s32[]{:S(2)}) async-start(), calls=%async_computation.1 | async-start | bytes 1572864 | tf_op jit(solution)/shard_map/while/body/eval_jaxpr/psum | solution.py:26
  739.3 25.3 %all-to-all-start = ((f32[32,32,192]{2,1,0:T(8,128)}), f32[32,32,192]{2,1,0:T(8,128)S(1)}, u32[]{:S(2)}, u32[]{:S(2)}) async-start(f32[32,32,192]{2,1,0:T(8,128)} %stack.7), calls=%async_computation | async-start | bytes 2097152 | tf_op jit(solution)/shard_map/while/body/eval_jaxpr/all_to_all | solution.py:32
  766.9 15.5 collective-permute-start
  782.3 145.2 %all-reduce.2.cloned.1.call-start = ((), (), s32[]{:S(2)}) async-start(), calls=%async_computation.1 | async-start | bytes 1572864 | tf_op jit(solution)/shard_map/while/body/eval_jaxpr/psum | solution.py:26
  930.7 25.3 %all-to-all-start = ((f32[32,32,192]{2,1,0:T(8,128)}), f32[32,32,192]{2,1,0:T(8,128)S(1)}, u32[]{:S(2)}, u32[]{:S(2)}) async-start(f32[32,32,192]{2,1,0:T(8,128)} %stack.7), calls=%async_computation | async-start | bytes 2097152 | tf_op jit(solution)/shard_map/while/body/eval_jaxpr/all_to_all | solution.py:32
  958.2 15.5 collective-permute-start
  973.7 145.2 %all-reduce.2.cloned.1.call-start = ((), (), s32[]{:S(2)}) async-start(), calls=%async_computation.1 | async-start | bytes 1572864 | tf_op jit(solution)/shard_map/while/body/eval_jaxpr/psum | solution.py:26
  1122.0 25.2 %all-to-all-start = ((f32[32,32,192]{2,1,0:T(8,128)}), f32[32,32,192]{2,1,0:T(8,128)S(1)}, u32[]{:S(2)}, u32[]{:S(2)}) async-start(f32[32,32,192]{2,1,0:T(8,128)} %stack.7), calls=%async_computation | async-start | bytes 2097152 | tf_op jit(solution)/shard_map/while/body/eval_jaxpr/all_to_all | solution.py:32
  1149.5 15.5 collective-permute-start
  1165.0 145.5 %all-reduce.2.cloned.1.call-start = ((), (), s32[]{:S(2)}) async-start(), calls=%async_computation.1 | async-start | bytes 1572864 | tf_op jit(solution)/shard_map/while/body/eval_jaxpr/psum | solution.py:26
  1313.6 25.3 %all-to-all-start = ((f32[32,32,192]{2,1,0:T(8,128)}), f32[32,32,192]{2,1,0:T(8,128)S(1)}, u32[]{:S(2)}, u32[]{:S(2)}) async-start(f32[32,32,192]{2,1,0:T(8,128)} %stack.7), calls=%async_computation | async-start | bytes 2097152 | tf_op jit(solution)/shard_map/while/body/eval_jaxpr/all_to_all | solution.py:32
  1341.2 15.5 collective-permute-start
  1356.6 145.5 %all-reduce.2.cloned.1.call-start = ((), (), s32[]{:S(2)}) async-start(), calls=%async_computation.1 | async-start | bytes 1572864 | tf_op jit(solution)/shard_map/while/body/eval_jaxpr/psum | solution.py:26
  1505.3 25.3 %all-to-all-start = ((f32[32,32,192]{2,1,0:T(8,128)}), f32[32,32,192]{2,1,0:T(8,128)S(1)}, u32[]{:S(2)}, u32[]{:S(2)}) async-start(f32[32,32,192]{2,1,0:T(8,128)} %stack.7), calls=%async_computation | async-start | bytes 2097152 | tf_op jit(solution)/shard_map/while/body/eval_jaxpr/all_to_all | solution.py:32
  1532.8 15.5 collective-permute-start
  1548.3 145.5 %all-reduce.2.cloned.1.call-start = ((), (), s32[]{:S(2)}) async-start(), calls=%async_computation.1 | async-start | bytes 1572864 | tf_op jit(solution)/shard_map/while/body/eval_jaxpr/psum | solution.py:26
  1696.9 25.3 %all-to-all-start = ((f32[32,32,192]{2,1,0:T(8,128)}), f32[32,32,192]{2,1,0:T(8,128)S(1)}, u32[]{:S(2)}, u32[]{:S(2)}) async-start(f32[32,32,192]{2,1,0:T(8,128)} %stack.7), calls=%async_computation | async-start | bytes 2097152 | tf_op jit(solution)/shard_map/while/body/eval_jaxpr/all_to_all | solution.py:32
  1724.4 15.5 collective-permute-start
  1739.9 145.2 %all-reduce.2.cloned.1.call-start = ((), (), s32[]{:S(2)}) async-start(), calls=%async_computation.1 | async-start | bytes 1572864 | tf_op jit(solution)/shard_map/while/body/eval_jaxpr/psum | solution.py:26
  1888.2 25.3 %all-to-all-start = ((f32[32,32,192]{2,1,0:T(8,128)}), f32[32,32,192]{2,1,0:T(8,128)S(1)}, u32[]{:S(2)}, u32[]{:S(2)}) async-start(f32[32,32,192]{2,1,0:T(8,128)} %stack.7), calls=%async_computation | async-start | bytes 2097152 | tf_op jit(solution)/shard_map/while/body/eval_jaxpr/all_to_all | solution.py:32
  1915.8 15.5 collective-permute-start
Sparse Core Ops, SparseCore 0:
  13.9 147.6 all-reduce.1
  212.0 141.2 all-reduce.1
  403.6 141.2 all-reduce.1
  594.9 141.2 all-reduce.1
  786.2 141.2 all-reduce.1
  977.5 141.2 all-reduce.1
  1169.2 141.2 all-reduce.1
  1360.8 141.2 all-reduce.1
  1552.5 141.2 all-reduce.1
  1743.8 141.2 all-reduce.1
